TPU v7x, 256 devices: a whole 4x4x8 slice. The times are simulated.
256 devices in a mesh: rep: 16 (over y, z_lo), tp: 16 (over z_hi, x, core).
Axes of the slice: x: 4, y: 4, z: 8 (z_hi: 2, z_lo: 4; z = z_hi * 4 + z_lo), core: 2. Of those that a mesh axis runs over, the one named last changes fastest.
Arguments:
- hidden_act: bfloat16 [16, 2048, 28672], P('rep', None, 'tp'), may hold values from -6 to 6
- out_grads: bfloat16 [16, 2048, 384], P('rep', 'tp'), may hold values from -0.125 to 0.125
- momentum: float32 [16, 28672, 384], P('rep', 'tp'), may hold values from -6 to 6
- coeff_index: int32 [16, 448, 6, 32], P(None, 'tp'), may hold values from 0 to 4095, as said below
Outputs:
- new_momentum: float32 [16, 28672, 384], P('rep', 'tp')
- update: bfloat16 [28672, 384], P('tp')
Inputs may be any that keep to these rules, and one draw needn't show every extreme that they name: `coeff_index`: the 32 indices of one block of one replica are distinct.
All inputs are finite; a program needn't handle non-finite values.
Results may differ from a plain program's by a relative error of at most 0.001.
Values may be sent and summed in bfloat16 or wider, within the bound.
A program may use at most 128 MiB of HBM per device.

v0:
```python
import jax
import jax.numpy as jnp
from jax import lax
from jax.sharding import PartitionSpec as P

SPAN = 64


decay_rate = 0.9


def dct_table():
    pos = jnp.arange(SPAN).astype(jnp.float32)
    freq = jnp.arange(SPAN).astype(jnp.float32)[:, None]
    scale = jnp.where(freq == 0.0, jnp.sqrt(1.0 / SPAN), jnp.sqrt(2.0 / SPAN)).astype(jnp.float32)
    return scale * jnp.cos(jnp.pi * (2.0 * pos[None, :] + 1.0) * freq / (2.0 * SPAN))


def forward_blocks(field, table):
    rows, cols = field.shape
    blocks = field.reshape(rows // SPAN, SPAN, cols // SPAN, SPAN)
    half = jnp.einsum("un,anbm->aubm", table, blocks, precision=lax.Precision.HIGHEST)
    return jnp.einsum("aubm,vm->aubv", half, table, precision=lax.Precision.HIGHEST)


def inverse_blocks(spectra, table):
    blocks_a, _, blocks_b, _ = spectra.shape
    half = jnp.einsum("un,aubv->anbv", table, spectra, precision=lax.Precision.HIGHEST)
    full = jnp.einsum("anbv,vm->anbm", half, table, precision=lax.Precision.HIGHEST)
    return full.reshape(blocks_a * SPAN, blocks_b * SPAN)


def per_device(hidden_act, out_grads, momentum, coeff_index):
    local_acts = hidden_act[0]
    rows = local_acts.shape[1]
    cols = out_grads.shape[2]
    blocks_a, blocks_b = (rows // SPAN, cols // SPAN)
    grad = jnp.einsum(
        "tf,tc->fc",
        local_acts,
        lax.all_gather(out_grads, "tp", axis=1, tiled=True)[0],
        preferred_element_type=jnp.float32,
    )
    mixed = decay_rate * momentum[0] + grad
    table = dct_table()
    spectrum = forward_blocks(mixed, table)
    own_index = lax.dynamic_index_in_dim(coeff_index, lax.axis_index("rep"), 0, keepdims=False)
    range_a = jnp.arange(blocks_a)[:, None, None]
    range_b = jnp.arange(blocks_b)[None, :, None]
    values = spectrum[range_a, own_index // SPAN, range_b, own_index % SPAN]
    sparse = (
        jnp.zeros(spectrum.shape, jnp.float32)
        .at[range_a, own_index // SPAN, range_b, own_index % SPAN]
        .add(values)
    )
    kept = inverse_blocks(sparse, table)
    new_moment = mixed - kept
    decoded = lax.psum(kept, "rep")
    blocks = decoded.reshape(blocks_a, SPAN, blocks_b, SPAN)
    meansq = jnp.mean(blocks * blocks, axis=(1, 3), keepdims=True)
    update = jnp.tanh(blocks / jnp.sqrt(meansq + 1e-06)).reshape(rows, cols).astype(jnp.bfloat16)
    return (new_moment[None], update)


def solution(mesh):
    placed = (
        P("rep", None, "tp"),
        P("rep", "tp", None),
        P("rep", "tp", None),
        P(None, "tp", None, None),
    )
    return jax.shard_map(
        per_device,
        mesh=mesh,
        in_specs=placed,
        out_specs=(P("rep", "tp", None), P("tp", None)),
        check_vma=False,
    )
```

profile of v0, /device:TPU:4, one launch (start us, length us, event | category | flops | bytes accessed | tf_op | source)
XLA Modules:
  0.0 458.2 jit_solution(12601315839904421965)
XLA Ops:
  7.2 0.0 all-gather.2.cloned.1.call-start
  7.2 0.7 all-gather.2.cloned.1.call-update
  7.9 2.4 or_reduce_fusion
  10.3 0.1 reshape.176
  10.5 1.3 multiply_reduce_fusion
  11.7 1.3 and_reduce_fusion
  13.1 0.1 reshape.182
  13.2 58.3 %all-gather.2.cloned.1.call-done = bf16[1,2048,384]{2,1,0:T(8,128)(2,1)} async-done(((bf16[1,128,384]{2,1,0:T(8,128)(2,1)}), bf16[1,2048,384]{2,1,0:T(8,128)(2,1)}) %all-gather.2.cloned.1.call-update) | async-done | bytes 1572880 | tf_op jit(solution)/shard_map/all_gather | solution.py:41
  71.5 8.5 %fusion.10 = f32[1792,384]{1,0:T(8,128)S(1)} fusion(bf16[1,2048,1792]{2,1,0:T(8,128)(2,1)} %param.4, f32[1,1792,384]{2,1,0:T(8,128)} %param.6, bf16[1,2048,384]{2,1,0:T(8,128)(2,1)} %all-gather.2.cloned.1.call-done), kind=kOutput, calls=%fused_computation.12 | convolution fusion | flops 2819948544 | bytes 14417920 | tf_op jit(solution)/shard_map/tf,tc->fc/dot_general | solution.py:38
  80.0 0.0 copy-start.2
  80.0 4.4 reshape.190
  84.4 0.0 copy-done.2
  84.4 8.8 %fusion.8 = f32[28,6,64,64]{2,3,1,0:T(8,128)S(1)} fusion(f32[28,64,6,64]{3,2,1,0:T(8,128)} %reshape.190, f32[64]{0:T(128)S(1)} %iota_convert_fusion, f32[64]{0:T(128)S(1)} %get-tuple-element.8, f32[64]{0:T(128)S(1)} %get-tuple-element.7), kind=kOutput, calls=%fused_computation.10 | convolution fusion | flops 528494592 | bytes 5505792 | tf_op jit(solution)/shard_map/un,anbm->aubm/dot_general | solution.py:22
  93.3 6.6 %fusion.6 = f32[28,64,6,64]{3,1,2,0:T(8,128)} fusion(f32[28,6,64,64]{2,3,1,0:T(8,128)S(1)} %fusion.8, f32[64]{0:T(128)S(1)} %iota_convert_fusion, f32[64]{0:T(128)S(1)} %get-tuple-element.8, f32[64]{0:T(128)S(1)} %get-tuple-element.7), kind=kOutput, calls=%fused_computation.8 | convolution fusion | flops 528494592 | bytes 5505792 | tf_op jit(solution)/shard_map/aubm,vm->aubv/dot_general | solution.py:23
  99.8 81.8 %gather_fusion = f32[5376]{0:T(1024)S(1)} fusion(f32[28,64,6,64]{3,1,2,0:T(8,128)} %fusion.6, s32[5376]{0:T(1024)S(1)} %reshape.176), kind=kCustom, calls=%fused_computation | custom fusion | bytes 129024 | tf_op jit(solution)/shard_map/gather | solution.py:50
  181.6 29.2 %scatter_custom_fusion = f32[688128]{0:T(1024)S(1)} fusion(s32[5376]{0:T(1024)S(1)} %reshape.182, f32[5376]{0:T(1024)S(1)} %gather_fusion, f32[]{:T(128)} %constant.57.clone.1), kind=kCustom, calls=%fused_computation.16 | custom fusion | flops 5376 | bytes 2752516
  210.9 3.4 reshape.174
  214.2 7.3 %fusion.4 = f32[28,6,64,64]{2,3,1,0:T(8,128)S(1)} fusion(f32[28,6,64,64]{3,2,1,0:T(8,128)} %reshape.174, f32[64]{0:T(128)S(1)} %iota_convert_fusion, f32[64]{0:T(128)S(1)} %get-tuple-element.8, f32[64]{0:T(128)S(1)} %get-tuple-element.7), kind=kOutput, calls=%fused_computation.6 | convolution fusion | flops 528494592 | bytes 5505792 | tf_op jit(solution)/shard_map/un,aubv->anbv/dot_general | solution.py:28
  221.5 6.6 %fusion.2 = f32[28,64,6,64]{3,1,2,0:T(8,128)} fusion(f32[28,6,64,64]{2,3,1,0:T(8,128)S(1)} %fusion.4, f32[64]{0:T(128)S(1)} %iota_convert_fusion, f32[64]{0:T(128)S(1)} %get-tuple-element.8, f32[64]{0:T(128)S(1)} %get-tuple-element.7), kind=kOutput, calls=%fused_computation.4 | convolution fusion | flops 528494592 | bytes 5505792 | tf_op jit(solution)/shard_map/anbv,vm->anbm/dot_general | solution.py:29
  228.0 7.0 %copy.8 = f32[28,64,6,64]{1,0,3,2:T(8,128)} copy(f32[28,64,6,64]{3,1,2,0:T(8,128)} %fusion.2) | data formatting | bytes 5505024 | tf_op jit(solution)/shard_map/anbv,vm->anbm/dot_general | solution.py:29
  235.1 4.4 reshape.171
  239.4 0.0 copy-start.1
  239.5 2.4 copy.9
  241.8 0.0 copy-done.1
  241.8 0.0 all-reduce.2.cloned.1.call-start
  241.8 0.0 copy-start.3
  241.8 0.7 all-reduce.2.cloned.1.call-update
  242.6 1.0 copy-done.3
  243.6 3.6 subtract_bitcast_fusion
  247.2 178.0 %all-reduce.2.cloned.1.call-done = f32[1792,384]{0,1:T(8,128)} async-done(((f32[1792,384]{0,1:T(8,128)}), f32[1792,384]{0,1:T(8,128)}) %all-reduce.2.cloned.1.call-update) | async-done | bytes 2752528 | tf_op jit(solution)/shard_map/psum | solution.py:58
  425.2 2.9 mul.112
  428.1 4.3 mul.113
  432.4 3.5 reduce_sum.9
  435.9 3.5 div.51
  439.4 0.0 copy-start
  439.4 5.8 %div.52 = f32[1792,384]{0,1:T(8,128)} reshape(f32[28,64,6,64]{1,0,3,2:T(8,128)} %div.51) | data formatting | bytes 5505024 | tf_op jit(solution)/shard_map/div | solution.py:61
  445.2 0.0 copy-done
  445.2 3.6 tanh_convert_fusion
  448.8 2.5 copy.10
  (6 shorter events, 0.1 us)
Async XLA Ops:
  7.2 64.3 %all-gather.2.cloned.1.call-start = ((), (), s32[]{:S(2)}) async-start(), calls=%async_computation | async-start | bytes 1671168 | tf_op jit(solution)/shard_map/all_gather | solution.py:41
  80.0 4.4 copy-start.2
  239.4 2.4 copy-start.1
  241.8 183.3 %all-reduce.2.cloned.1.call-start = ((), (), s32[]{:S(2)}) async-start(), calls=%async_computation.1 | async-start | bytes 5505024 | tf_op jit(solution)/shard_map/psum | solution.py:58
  241.8 1.8 copy-start.3
  439.4 5.8 %copy-start = (f32[1792,384]{0,1:T(8,128)S(1)}, f32[1792,384]{0,1:T(8,128)}, u32[]{:S(2)}) copy-start(f32[1792,384]{0,1:T(8,128)} %all-reduce.2.cloned.1.call-done) | copy-start | bytes 8257540
Sparse Core Ops, SparseCore 0:
  10.7 60.6 all-gather.1
  245.3 179.7 all-reduce.1
where the time goes:
time: 461 us; the launch traced here: 458 us
  waiting for transfers between devices  238 us (52%)
  local copies, waits for them, and re-layouts  121 us (26%)
  other arithmetic  47.8 us (10%)
  matrix products  37.7 us (8%)
  between operations  14.2 us (3%)
    psum x1, waiting for transfers between devices, per_device(): decoded = lax.psum(kept, 'rep')  178 us
    gather x1, local copies, waits for them, and re-layouts, per_device(): values = spectrum[range_a, own_index // SPAN, range_b, own_index % SPAN]  81.8 us
    all_gather x1, waiting for transfers between devices, per_device(): lax.all_gather(out_grads, 'tp', axis=1, tiled=True)[0]  58.3 us
    unnamed x4, other arithmetic  31.8 us
    div x2, local copies, waits for them, and re-layouts, per_device(): blocks / jnp.sqrt(meansq + 1e-06)  9.37 us
  transfers between devices with their start and end apart: 2, of which 2 were waited for; matrix products, arithmetic and copies ran while one was open for 2% of the time, Pallas kernels for 0%

commit v1 on v0

v1 whole, which is shorter than its diff:
```python
import functools

import jax
import jax.numpy as jnp
import ml_dtypes
import numpy as np
from jax import lax
from jax.experimental import pallas as pl
from jax.experimental.pallas import tpu as pltpu
from jax.sharding import PartitionSpec as P

SPAN = 64
DECAY = 0.9
MESH = pl.DeviceIdType.MESH
f32, bf16, i32 = jnp.float32, jnp.bfloat16, jnp.int32


def dct_table():
    n = np.arange(SPAN)
    u = np.arange(SPAN)[:, None]
    scale = np.where(u == 0, np.sqrt(1.0 / SPAN), np.sqrt(2.0 / SPAN))
    return (scale * np.cos(np.pi * (2 * n[None] + 1) * u / (2 * SPAN))).astype(np.float32)


def split_table(x):
    high = x.astype(ml_dtypes.bfloat16)
    low = (x - high.astype(np.float32)).astype(ml_dtypes.bfloat16)
    return high, low


def split(x):
    high = x.astype(bf16)
    return high, (x - high.astype(f32)).astype(bf16)


def dot(a, b):
    return jnp.dot(a, b, preferred_element_type=f32)


def dot_t(a, b):
    return lax.dot_general(a, b, (((1,), (1,)), ((), ())), preferred_element_type=f32)


def dot3(ah, al, bh, bl):
    return dot(ah, bh) + dot(al, bh) + dot(ah, bl)


def lane_gather(x, idx):
    return jnp.take_along_axis(x, idx, axis=1, mode="promise_in_bounds")


def exchange_kernel(
    og_hbm, act_hbm, mom_hbm, idx_hbm, dth, dtl, ct2,
    newmom_hbm, vals, iu, iv,
    act, og, gt, mixed, idx, cu, rh, rl, wrow,
    load_sem, og_send, og_recv, v_send, v_recv, out_sem,
):
    rep, tp = lax.axis_index("rep"), lax.axis_index("tp")
    y, zl = rep // 4, rep % 4
    zh, x, c = tp // 8, (tp // 2) % 4, tp % 2
    tok = og_hbm.shape[1]

    def tpid(zh_, x_, c_):
        return (zh_ * 4 + x_) * 2 + c_

    xs = [lax.rem(x + 1, 4), lax.rem(x + 3, 4), lax.rem(x + 2, 4)]
    x_peers = [tpid(zh, xx, c) for xx in xs]
    core_peer = tpid(zh, x, 1 - c)
    z_peer = tpid(1 - zh, x, c)
    z_reps = [y * 4 + lax.rem(zl + d, 4) for d in (1, 2, 3)]
    y_reps = [lax.rem(y + d, 4) * 4 + zl for d in (1, 3, 2)]

    loads = []

    def load(src, dst):
        cp = pltpu.make_async_copy(src, dst, load_sem.at[len(loads)])
        cp.start()
        loads.append(cp)
        return cp

    def slot(t):
        return pl.ds(pl.multiple_of(t * tok, tok), tok)

    og_in = load(og_hbm.at[0], og.at[slot(tp)])
    idx_in = load(idx_hbm, idx)
    half = 4 * 2 * tok
    act_in = []
    for h in (zh, 1 - zh):
        rows = pl.ds(pl.multiple_of(h * half, half), half)
        act_in.append(load(act_hbm.at[0, rows], act.at[rows]))
    mom_in = load(mom_hbm.at[0], mixed)

    barrier = pltpu.get_barrier_semaphore()
    for t in x_peers + [core_peer, z_peer]:
        pl.semaphore_signal(barrier, inc=1, device_id=(rep, t), device_id_type=MESH)
    for r in z_reps + y_reps:
        pl.semaphore_signal(barrier, inc=1, device_id=(r, tp), device_id_type=MESH)
    pl.semaphore_wait(barrier, 11)

    sends = []

    def send(src_tp, dst_tp):
        cp = pltpu.make_async_remote_copy(
            src_ref=og.at[slot(src_tp)],
            dst_ref=og.at[slot(src_tp)],
            send_sem=og_send.at[len(sends)],
            recv_sem=og_recv.at[src_tp],
            device_id=(rep, dst_tp),
            device_id_type=MESH,
        )
        cp.start()
        sends.append(cp)

    def arrived(src_tp):
        pltpu.make_async_remote_copy(
            src_ref=og.at[slot(src_tp)],
            dst_ref=og.at[slot(src_tp)],
            send_sem=og_send.at[0],
            recv_sem=og_recv.at[src_tp],
            device_id=(rep, tp),
            device_id_type=MESH,
        ).wait_recv()

    og_in.wait()
    send(tp, z_peer)
    for t in x_peers:
        send(tp, t)
    send(tp, core_peer)

    idx_in.wait()

    def index_rows(a, _):
        for g in range(4):
            row = jnp.concatenate([idx[4 * g + i, a] for i in range(4)], axis=1)
            iu[a, g, 0:6, :] = (row >> 6).astype(f32)
            iv[a, g, 0:6, :] = (row & 63).astype(f32)
        return 0

    lax.fori_loop(0, 28, index_rows, 0)

    def own_tables(j, _):
        row_b = lax.broadcasted_iota(i32, (128, 128), 0) // 64
        lane = lax.broadcasted_iota(i32, (128, 128), 1)
        mine = row_b == (lane // 32) % 2
        for q in range(6):
            a2, bp = q // 3, q % 3
            row = jnp.concatenate(
                [idx[rep, 4 * j + 2 * a2 + ap, 2 * bp + b : 2 * bp + b + 1, :] for ap in range(2) for b in range(2)],
                axis=1,
            )
            k = j * 6 + q
            cu[k] = lane_gather(ct2[...], jnp.broadcast_to(row >> 6, (64, 128)))
            cv = lane_gather(ct2[...], jnp.broadcast_to(row & 63, (64, 128)))
            cvh, cvl = split(jnp.where(mine, jnp.concatenate([cv, cv], axis=0), 0.0))
            rh[k] = cvh
            rl[k] = cvl
        return 0

    lax.fori_loop(0, 7, own_tables, 0)

    for t in x_peers:
        arrived(t)
        send(t, core_peer)
    arrived(z_peer)
    for t in x_peers:
        send(z_peer, t)
    send(z_peer, core_peer)

    arrived(core_peer)
    for xx in xs:
        arrived(tpid(zh, xx, 1 - c))
    act_in[0].wait()

    def partial_grad(off, depth, first):
        off = pl.multiple_of(off, depth)
        bt = og[pl.ds(off, depth), :].T

        def body(j, _):
            cols = pl.ds(pl.multiple_of(j * 256, 256), 256)
            part = dot(bt, act[pl.ds(off, depth), cols])
            gt[:, cols] = part if first else gt[:, cols] + part
            return 0

        lax.fori_loop(0, 7, body, 0)

    partial_grad(zh * half, half, True)

    for xx in xs:
        t = tpid(1 - zh, xx, c)
        arrived(t)
        send(t, core_peer)
    act_in[1].wait()
    mom_in.wait()
    arrived(tpid(1 - zh, x, 1 - c))
    for xx in xs:
        arrived(tpid(1 - zh, xx, 1 - c))

    off2 = pl.multiple_of((1 - zh) * half, half)
    bt2 = og[pl.ds(off2, half), :].T

    def forward(j, _):
        cols = pl.ds(pl.multiple_of(j * 256, 256), 256)
        g = gt[:, cols] + dot(bt2, act[pl.ds(off2, half), cols])
        m = DECAY * mixed[cols, :] + g.T
        mixed[cols, :] = m
        mh, ml = split(m)
        lane = lax.broadcasted_iota(i32, (64, 128), 1)
        ws = []
        hs = [dot3(mh[:, :256], ml[:, :256], dth[...], dtl[...])]
        hs.append(dot3(mh[:, 256:], ml[:, 256:], dth[:128, :128], dtl[:128, :128]))
        hs = [hs[0][:, :128], hs[0][:, 128:], hs[1]]
        for q in range(6):
            a2, bp = q // 3, q % 3
            row = jnp.concatenate(
                [
                    (idx[rep, 4 * j + 2 * a2 + ap, 2 * bp + b : 2 * bp + b + 1, :] & 63) + 64 * b
                    for ap in range(2)
                    for b in range(2)
                ],
                axis=1,
            )
            ib = jnp.broadcast_to(row, (64, 128))
            h = hs[bp][128 * a2 : 128 * a2 + 128]
            got = jnp.where(lane < 64, lane_gather(h[:64], ib), lane_gather(h[64:], ib))
            w = jnp.sum(got * cu[j * 6 + q], axis=0, keepdims=True)
            wrow[pl.ds(j * 6 + q, 1), :] = w
            ws.append(w)
        rows = []
        for b in range(6):
            bp, bo = b // 2, 32 * (b % 2)
            rows.append(
                jnp.concatenate([ws[3 * a2 + bp][:, o + bo : o + bo + 32] for a2 in range(2) for o in (0, 64)], axis=1)
            )
        vals[rep, j] = jnp.concatenate(rows + [jnp.zeros((2, 128), f32)], axis=0)
        return 0

    def vcopy(r, to, lo, n, si, ri):
        return pltpu.make_async_remote_copy(
            src_ref=vals.at[r, pl.ds(lo, n)],
            dst_ref=vals.at[r, pl.ds(lo, n)],
            send_sem=v_send.at[si],
            recv_sem=v_recv.at[r, ri],
            device_id=(to, tp),
            device_id_type=MESH,
        )

    groups = [(0, 4), (4, 3)]
    vsends = []

    def vsend(r, to, gi):
        cp = vcopy(r, to, *groups[gi], len(vsends), gi)
        cp.start()
        vsends.append(cp)

    def varrived(r, gi):
        vcopy(r, rep, *groups[gi], 0, gi).wait_recv()

    lax.fori_loop(0, 4, forward, 0)
    for r in z_reps + y_reps:
        vsend(rep, r, 0)
    lax.fori_loop(4, 7, forward, 0)
    for r in z_reps + y_reps:
        vsend(rep, r, 1)
    for z in z_reps:
        varrived(z, 0)
        for r in y_reps:
            vsend(z, r, 0)

    outs = []

    def keep(j, _):
        lane = lax.broadcasted_iota(i32, (64, 128), 1)
        for q in range(6):
            a2, bp = q // 3, q % 3
            k = j * 6 + q
            l = cu[k] * jnp.broadcast_to(wrow[pl.ds(k, 1), :], (64, 128))
            lh, ll = split(jnp.concatenate([jnp.where(lane < 64, l, 0.0), jnp.where(lane < 64, 0.0, l)], axis=0))
            kept = dot_t(lh, rh[k]) + dot_t(ll, rh[k]) + dot_t(lh, rl[k])
            rows = pl.ds(pl.multiple_of(j * 256 + a2 * 128, 128), 128)
            cols = slice(bp * 128, bp * 128 + 128)
            mixed[rows, cols] = mixed[rows, cols] - kept
        return 0

    def write(lo, n):
        rows = pl.ds(lo * 256, n * 256)
        cp = pltpu.make_async_copy(mixed.at[rows], newmom_hbm.at[rows], out_sem.at[len(outs)])
        cp.start()
        outs.append(cp)

    lax.fori_loop(0, 4, keep, 0)
    write(0, 4)
    for z in z_reps:
        varrived(z, 1)
        for r in y_reps:
            vsend(z, r, 1)
    lax.fori_loop(4, 7, keep, 0)
    write(4, 3)

    for yr in y_reps:
        for gi in range(2):
            varrived(yr, gi)
        for d in (1, 2, 3):
            for gi in range(2):
                varrived((yr // 4) * 4 + lax.rem(zl + d, 4), gi)
    for cp in sends + vsends:
        cp.wait_send()
    for cp in outs:
        cp.wait()


def exchange(og, act, mom, idx):
    rows, cols = mom.shape[1:]
    tok = act.shape[1]
    table = dct_table()
    dth, dtl = split_table(np.kron(np.eye(4, dtype=np.float32), table.T))
    ct2 = np.concatenate([table.T, table.T], axis=1)
    vmem = pl.BlockSpec(memory_space=pltpu.VMEM)
    anyw = pl.BlockSpec(memory_space=pl.ANY)
    S = jax.ShapeDtypeStruct
    return pl.pallas_call(
        exchange_kernel,
        out_shape=(
            S((rows, cols), f32),
            S((16, 7, 8, 128), f32),
            S((28, 4, 8, 128), f32),
            S((28, 4, 8, 128), f32),
        ),
        in_specs=[anyw] * 4 + [vmem] * 3,
        out_specs=(anyw, vmem, vmem, vmem),
        scratch_shapes=[
            pltpu.VMEM((tok, rows), bf16),
            pltpu.VMEM((tok, cols), bf16),
            pltpu.VMEM((cols, rows), f32),
            pltpu.VMEM((rows, cols), f32),
            pltpu.VMEM(idx.shape, i32),
            pltpu.VMEM((42, 64, 128), f32),
            pltpu.VMEM((42, 128, 128), bf16),
            pltpu.VMEM((42, 128, 128), bf16),
            pltpu.VMEM((48, 128), f32),
            pltpu.SemaphoreType.DMA((5,)),
            pltpu.SemaphoreType.DMA((16,)),
            pltpu.SemaphoreType.DMA((16,)),
            pltpu.SemaphoreType.DMA((32,)),
            pltpu.SemaphoreType.DMA((16, 2)),
            pltpu.SemaphoreType.DMA((2,)),
        ],
        compiler_params=pltpu.CompilerParams(collective_id=0, has_side_effects=True, vmem_limit_bytes=56 << 20),
        name="exchange",
    )(og, act, mom, idx, dth, dtl, ct2)


def decode_kernel(
    newmom_in, vals, iu, iv, dth, dtl, dch, dcl, newmom, update, s_buf, v_buf, sem
):
    cp = pltpu.make_async_copy(newmom_in, newmom.at[0], sem)
    cp.start()
    io = lax.broadcasted_iota(i32, (64, 128), 0).astype(f32).astype(bf16)
    io2 = lax.broadcasted_iota(i32, (128, 128), 0).astype(f32).astype(bf16)
    zero, zero2 = jnp.zeros((64, 128), bf16), jnp.zeros((128, 128), bf16)
    one2 = jnp.ones((128, 128), bf16)

    def spread(row, n):
        return jnp.broadcast_to(row, (n, 128)).astype(bf16)

    def body(j, _):
        for g in range(4):
            got = [vals[4 * g + i, j] for i in range(4)]
            for ai in range(4):
                v_buf[ai, g] = jnp.concatenate([v[:, 32 * ai : 32 * ai + 32] for v in got], axis=1)
        for ai in range(4):
            for bp in range(3):
                left, right = [], []
                for bo in range(2):
                    b = 2 * bp + bo
                    for g in range(4):
                        hit = spread(iu[4 * j + ai, g, b : b + 1, :], 64) == io
                        v = v_buf[ai, g, b : b + 1, :]
                        vh = v.astype(bf16).astype(f32)
                        left.append(
                            jnp.concatenate(
                                [jnp.where(hit, spread(vh, 64), zero), jnp.where(hit, spread(v - vh, 64), zero)], axis=0
                            )
                        )
                        at = spread(iv[4 * j + ai, g, b : b + 1, :] + 64.0 * bo, 128)
                        right.append(jnp.where(at == io2, one2, zero2))
                o = dot_t(jnp.concatenate(left, axis=1), jnp.concatenate(right, axis=1))
                s_buf[64 * ai : 64 * ai + 64, 128 * bp : 128 * bp + 128] = o[:64] + o[64:]
        sh, sl = split(s_buf[...])
        t = jnp.concatenate(
            [
                dot3(sh[:, :256], sl[:, :256], dch[...], dcl[...]),
                dot3(sh[:, 256:], sl[:, 256:], dch[:128, :128], dcl[:128, :128]),
            ],
            axis=1,
        )
        th, tl = split(t)
        d = dot3(dth[...], dtl[...], th, tl)
        lane = lax.broadcasted_iota(i32, (1, 128), 1)
        for ai in range(4):
            for bp in range(3):
                blk = d[64 * ai : 64 * ai + 64, 128 * bp : 128 * bp + 128]
                col = jnp.sum(blk * blk, axis=0, keepdims=True)
                lo = jnp.sum(jnp.where(lane < 64, col, 0.0), axis=1, keepdims=True)
                hi = jnp.sum(jnp.where(lane < 64, 0.0, col), axis=1, keepdims=True)
                q = jnp.where(lane < 64, lo, hi) * (1.0 / (SPAN * SPAN))
                update[pl.ds(pl.multiple_of(j * 256 + 64 * ai, 64), 64), 128 * bp : 128 * bp + 128] = jnp.tanh(
                    blk * lax.rsqrt(q + 1e-06)
                ).astype(bf16)
        return 0

    lax.fori_loop(0, 7, body, 0)
    cp.wait()


def decode(newmom, vals, iu, iv):
    rows, cols = newmom.shape
    table = dct_table()
    dt = np.kron(np.eye(4, dtype=np.float32), table.T)
    dth, dtl = split_table(dt)
    dch, dcl = split_table(dt.T.copy())
    vmem = pl.BlockSpec(memory_space=pltpu.VMEM)
    anyw = pl.BlockSpec(memory_space=pl.ANY)
    S = jax.ShapeDtypeStruct
    return pl.pallas_call(
        decode_kernel,
        out_shape=(S((1, rows, cols), f32), S((rows, cols), bf16)),
        in_specs=[anyw] + [vmem] * 7,
        out_specs=(anyw, vmem),
        scratch_shapes=[
            pltpu.VMEM((256, cols), f32),
            pltpu.VMEM((4, 4, 8, 128), f32),
            pltpu.SemaphoreType.DMA,
        ],
        compiler_params=pltpu.CompilerParams(vmem_limit_bytes=56 << 20),
        name="decode",
    )(newmom, vals, iu, iv, dth, dtl, dch, dcl)


def per_device(hidden_act, out_grads, momentum, coeff_index):
    newmom, vals, iu, iv = exchange(out_grads, hidden_act, momentum, coeff_index)
    return decode(newmom, vals, iu, iv)


def solution(mesh):
    placed = (
        P("rep", None, "tp"),
        P("rep", "tp", None),
        P("rep", "tp", None),
        P(None, "tp", None, None),
    )
    return jax.shard_map(
        per_device,
        mesh=mesh,
        in_specs=placed,
        out_specs=(P("rep", "tp", None), P("tp", None)),
        check_vma=False,
    )
```

time: 461 us -> 132 us (0.29)
  the two profiles are of different devices: /device:TPU:4 before, /device:TPU:1 now
where the time goes in v1:
time: 132 us
  Pallas kernels  128 us (97%)
  local copies, waits for them, and re-layouts  3.02 us (2%)
    pallas_call x1, Pallas kernels, decode(): pl.pallas_call(decode_kernel, out_shape=(S((1, rows, cols), f32), S((rows...  87 us
    pallas_call x1, Pallas kernels, exchange(): pl.pallas_call(exchange_kernel, out_shape=(S((rows, cols), f32), S((16, 7...  41.3 us
    unnamed x1, local copies, waits for them, and re-layouts  3.02 us

profile of v1, /device:TPU:1, one launch (start us, length us, event | category | flops | bytes accessed | tf_op | source)
XLA Modules:
  0.0 132.0 jit_solution(12253096615010284598)
XLA Ops:
  0.6 3.0 %copy.13.idx_hbm = s32[16,28,6,32]{3,2,1,0:T(8,128)} copy(s32[16,28,6,32]{3,0,2,1:T(8,128)} %param.14) | data formatting | bytes 688128 | tf_op args[3]
  3.6 41.3 %exchange.1 = (f32[1792,384]{1,0:T(8,128)}, f32[16,7,8,128]{3,2,1,0:T(8,128)}, f32[28,4,8,128]{3,2,1,0:T(8,128)}, f32[28,4,8,128]{3,2,1,0:T(8,128)}) custom-call(bf16[1,128,384]{2,1,0:T(8,128)(2,1)} %og_hbm.1, bf16[1,2048,1792]{2,1,0:T(8,128)(2,1)} %act_hbm.1, f32[1,1792,384]{2,1,0:T(8,128)} %mom_hbm.1, s32[16,28,6,32]{3,2,1,0:T(8,128)} %copy.13.idx_hbm, ...), custom_call_target="tpu_custom_call" | custom-call | tf_op jit(solution)/shard_map/exchange/pallas_call | solution.py:320
  45.0 87.0 %decode.1 = (f32[1,1792,384]{2,1,0:T(8,128)}, bf16[1792,384]{1,0:T(8,128)(2,1)}) custom-call(f32[1792,384]{1,0:T(8,128)} %get-tuple-element.6.newmom_in, f32[16,7,8,128]{3,2,1,0:T(8,128)} %get-tuple-element.7.vals, f32[28,4,8,128]{3,2,1,0:T(8,128)} %get-tuple-element.8.iu, f32[28,4,8,128]{3,2,1,0:T(8,128)} %get-tuple-element.9.iv, ...), custom_call_target="tpu_custom_call" | custom-call | tf_op jit(solution)/shard_map/decode/pallas_call | solution.py:424

commit v2 on v1

v2 whole, which is shorter than its diff:
```python
import functools

import jax
import jax.numpy as jnp
import ml_dtypes
import numpy as np
from jax import lax
from jax.experimental import pallas as pl
from jax.experimental.pallas import tpu as pltpu
from jax.sharding import PartitionSpec as P

SPAN = 64
DECAY = 0.9
PIECES = 4
EARLY = 2
MESH = pl.DeviceIdType.MESH
f32, bf16, i32 = jnp.float32, jnp.bfloat16, jnp.int32


def dct_table():
    n = np.arange(SPAN)
    u = np.arange(SPAN)[:, None]
    scale = np.where(u == 0, np.sqrt(1.0 / SPAN), np.sqrt(2.0 / SPAN))
    return (scale * np.cos(np.pi * (2 * n[None] + 1) * u / (2 * SPAN))).astype(np.float32)


def split_table(x):
    high = x.astype(ml_dtypes.bfloat16)
    low = (x - high.astype(np.float32)).astype(ml_dtypes.bfloat16)
    return high, low


def split(x):
    high = x.astype(bf16)
    return high, (x - high.astype(f32)).astype(bf16)


def dot(a, b):
    return jnp.dot(a, b, preferred_element_type=f32)


def dot_t(a, b):
    return lax.dot_general(a, b, (((1,), (1,)), ((), ())), preferred_element_type=f32)


def dot3(ah, al, bh, bl):
    return dot(ah, bh) + dot(al, bh) + dot(ah, bl)


def lane_gather(x, idx):
    return jnp.take_along_axis(x, idx, axis=1, mode="promise_in_bounds")


def exchange_kernel(
    og_hbm, act_hbm, mom_hbm, idx_hbm, dth_hbm, dtl_hbm, dch_hbm, dcl_hbm, ct2_hbm,
    newmom_hbm, upd_hbm, vals, iuv,
    act, og, gt, mixed, idx, cu, rh, rl, wrow, dth, dtl, dch, dcl, ct2, upd, s_a, s_b, v_a, v_b,
    load_sem, og_send, og_recv, core_recv, v_send, v_recv, out_sem,
):
    rep, tp = lax.axis_index("rep"), lax.axis_index("tp")
    y, zl = rep // 4, rep % 4
    zh, x, c = tp // 8, (tp // 2) % 4, tp % 2
    tok = og_hbm.shape[1]

    def tpid(zh_, x_, c_):
        return (zh_ * 4 + x_) * 2 + c_

    xs = [lax.rem(x + 1, 4), lax.rem(x + 3, 4), lax.rem(x + 2, 4)]
    x_peers = [tpid(zh, xx, c) for xx in xs]
    core_peer = tpid(zh, x, 1 - c)
    z_peer = tpid(1 - zh, x, c)
    z_reps = [y * 4 + lax.rem(zl + d, 4) for d in (1, 2, 3)]
    y_reps = [lax.rem(y + d, 4) * 4 + zl for d in (1, 3, 2)]
    far_reps = [lax.rem(y + d, 4) * 4 + lax.rem(zl + e, 4) for d in (1, 3, 2) for e in (1, 2, 3)]
    all_reps = z_reps + y_reps + far_reps

    barrier = pltpu.get_barrier_semaphore()
    for t in x_peers + [core_peer, z_peer]:
        pl.semaphore_signal(barrier, inc=1, device_id=(rep, t), device_id_type=MESH)
    for r in all_reps:
        pl.semaphore_signal(barrier, inc=1, device_id=(r, tp), device_id_type=MESH)

    loads = []

    def load(src, dst):
        cp = pltpu.make_async_copy(src, dst, load_sem.at[len(loads)])
        cp.start()
        loads.append(cp)
        return cp

    def slot(t):
        return pl.ds(pl.multiple_of(t * tok, tok), tok)

    og_in = load(og_hbm.at[0], og.at[slot(tp)])
    idx_in = load(idx_hbm, idx)
    ct2_in = load(ct2_hbm, ct2)
    half = 4 * 2 * tok
    act_in = []
    for h in (zh, 1 - zh):
        rows = pl.ds(pl.multiple_of(h * half, half), half)
        act_in.append(load(act_hbm.at[0, rows], act.at[rows]))
    mom_in = load(mom_hbm.at[0], mixed)
    table_in = [load(dth_hbm, dth), load(dtl_hbm, dtl), load(dch_hbm, dch), load(dcl_hbm, dcl)]

    pl.semaphore_wait(barrier, 5 + len(all_reps))

    sends = []
    size = tok // PIECES

    def piece_copy(src_tp, dst_tp, p, k):
        rows = pl.ds(pl.multiple_of(src_tp * tok + p * size, size), size)
        return pltpu.make_async_remote_copy(
            src_ref=og.at[rows],
            dst_ref=og.at[rows],
            send_sem=og_send.at[k],
            recv_sem=og_recv.at[src_tp, p],
            device_id=(rep, dst_tp),
            device_id_type=MESH,
        )

    def core_copy(src_tp, k):
        return pltpu.make_async_remote_copy(
            src_ref=og.at[slot(src_tp)],
            dst_ref=og.at[slot(src_tp)],
            send_sem=og_send.at[k],
            recv_sem=core_recv.at[src_tp],
            device_id=(rep, core_peer),
            device_id_type=MESH,
        )

    def send(src_tp, dst_tp, p):
        cp = piece_copy(src_tp, dst_tp, p, len(sends))
        cp.start()
        sends.append(cp)

    def send_core(src_tp):
        cp = core_copy(src_tp, len(sends))
        cp.start()
        sends.append(cp)

    def arrived(src_tp, p):
        piece_copy(src_tp, tp, p, 0).wait_recv()

    def arrived_core(src_tp):
        core_copy(src_tp, 0).wait_recv()

    og_in.wait()
    for p in range(PIECES):
        send(tp, z_peer, p)
        for t in x_peers:
            send(tp, t, p)
    send_core(tp)

    idx_in.wait()
    ct2_in.wait()

    def index_rows(a, _):
        for b in range(6):
            got = idx[a, b]
            row = jnp.concatenate([got[4 * i : 4 * i + 4] for i in range(4)], axis=1)
            iuv[a, b] = jnp.concatenate([row >> 6, row & 63], axis=0).astype(f32)
        return 0

    lax.fori_loop(0, 28, index_rows, 0)

    def own_tables(j, _):
        row_b = lax.broadcasted_iota(i32, (128, 128), 0) // 64
        lane = lax.broadcasted_iota(i32, (128, 128), 1)
        mine = row_b == (lane // 32) % 2
        for q in range(6):
            a2, bp = q // 3, q % 3
            row = jnp.concatenate(
                [idx[4 * j + 2 * a2 + ap, 2 * bp + b, pl.ds(rep, 1), :] for ap in range(2) for b in range(2)],
                axis=1,
            )
            k = j * 6 + q
            cu[k] = lane_gather(ct2[...], jnp.broadcast_to(row >> 6, (64, 128)))
            cv = lane_gather(ct2[...], jnp.broadcast_to(row & 63, (64, 128)))
            cvh, cvl = split(jnp.where(mine, jnp.concatenate([cv, cv], axis=0), 0.0))
            rh[k] = cvh
            rl[k] = cvl
        return 0

    for p in range(PIECES):
        arrived(z_peer, p)
        for t in x_peers:
            send(z_peer, t, p)
        lax.fori_loop(7 * p // PIECES, 7 * (p + 1) // PIECES, own_tables, 0)
    send_core(z_peer)
    for t in x_peers:
        for p in range(PIECES):
            arrived(t, p)
        send_core(t)

    arrived_core(core_peer)
    for xx in xs:
        arrived_core(tpid(zh, xx, 1 - c))
    act_in[0].wait()

    def partial_grad(off, depth, first):
        off = pl.multiple_of(off, depth)
        bt = og[pl.ds(off, depth), :].T

        def body(j, _):
            cols = pl.ds(pl.multiple_of(j * 256, 256), 256)
            part = dot(bt, act[pl.ds(off, depth), cols])
            gt[:, cols] = part if first else gt[:, cols] + part
            return 0

        lax.fori_loop(0, 7, body, 0)

    partial_grad(zh * half, half, True)

    for xx in xs:
        t = tpid(1 - zh, xx, c)
        for p in range(PIECES):
            arrived(t, p)
        send_core(t)
    act_in[1].wait()
    mom_in.wait()
    for cp in table_in:
        cp.wait()
    arrived_core(tpid(1 - zh, x, 1 - c))
    for xx in xs:
        arrived_core(tpid(1 - zh, xx, 1 - c))

    off2 = pl.multiple_of((1 - zh) * half, half)
    bt2 = og[pl.ds(off2, half), :].T

    def forward(j):
        cols = slice(j * 256, j * 256 + 256)
        g = gt[:, cols] + dot(bt2, act[pl.ds(off2, half), cols])
        m = DECAY * mixed[cols, :] + g.T
        mixed[cols, :] = m
        mh, ml = split(m)
        lane = lax.broadcasted_iota(i32, (64, 128), 1)
        ws = []
        hs = [dot3(mh[:, :256], ml[:, :256], dth[...], dtl[...])]
        hs.append(dot3(mh[:, 256:], ml[:, 256:], dth[:128, :128], dtl[:128, :128]))
        hs = [hs[0][:, :128], hs[0][:, 128:], hs[1]]
        for q in range(6):
            a2, bp = q // 3, q % 3
            row = jnp.concatenate(
                [
                    (idx[4 * j + 2 * a2 + ap, 2 * bp + b, pl.ds(rep, 1), :] & 63) + 64 * b
                    for ap in range(2)
                    for b in range(2)
                ],
                axis=1,
            )
            ib = jnp.broadcast_to(row, (64, 128))
            h = hs[bp][128 * a2 : 128 * a2 + 128]
            got = jnp.where(lane < 64, lane_gather(h[:64], ib), lane_gather(h[64:], ib))
            w = jnp.sum(got * cu[j * 6 + q], axis=0, keepdims=True)
            wrow[j * 6 + q : j * 6 + q + 1, :] = w
            ws.append(w)
        rows = []
        for b in range(6):
            bp, bo = b // 2, 32 * (b % 2)
            rows.append(
                jnp.concatenate([ws[3 * a2 + bp][:, o + bo : o + bo + 32] for a2 in range(2) for o in (0, 64)], axis=1)
            )
        vals[rep, j] = jnp.concatenate(rows + [jnp.zeros((2, 128), f32)], axis=0)

    def vcopy(r, to, lo, n, si, ri):
        return pltpu.make_async_remote_copy(
            src_ref=vals.at[r, pl.ds(lo, n)],
            dst_ref=vals.at[r, pl.ds(lo, n)],
            send_sem=v_send.at[si],
            recv_sem=v_recv.at[r, ri],
            device_id=(to, tp),
            device_id_type=MESH,
        )

    groups = [(0, 4), (4, 2), (6, 1)]
    vsends = []

    def vsend(r, to, gi):
        cp = vcopy(r, to, *groups[gi], len(vsends), gi)
        cp.start()
        vsends.append(cp)

    def varrived(r, gi):
        vcopy(r, rep, *groups[gi], 0, gi).wait_recv()

    for j in range(4):
        forward(j)
    for r in z_reps + y_reps:
        vsend(rep, r, 0)
    for j in range(4, 6):
        forward(j)
    for r in z_reps + y_reps:
        vsend(rep, r, 1)
    for z in z_reps:
        varrived(z, 0)
        for r in y_reps:
            vsend(z, r, 0)
    forward(6)
    for r in all_reps:
        vsend(rep, r, 2)

    outs = []

    def keep(j):
        lane = lax.broadcasted_iota(i32, (64, 128), 1)
        for q in range(6):
            a2, bp = q // 3, q % 3
            k = j * 6 + q
            l = cu[k] * jnp.broadcast_to(wrow[k : k + 1, :], (64, 128))
            lh, ll = split(jnp.concatenate([jnp.where(lane < 64, l, 0.0), jnp.where(lane < 64, 0.0, l)], axis=0))
            kept = dot_t(lh, rh[k]) + dot_t(ll, rh[k]) + dot_t(lh, rl[k])
            rows = slice(j * 256 + a2 * 128, j * 256 + a2 * 128 + 128)
            cols = slice(bp * 128, bp * 128 + 128)
            mixed[rows, cols] = mixed[rows, cols] - kept

    def write(src, dst, lo, n):
        rows = pl.ds(lo * 256, n * 256)
        cp = pltpu.make_async_copy(src.at[rows], dst.at[rows], out_sem.at[len(outs)])
        cp.start()
        outs.append(cp)

    for j in range(4):
        keep(j)
    write(mixed, newmom_hbm, 0, 4)
    for z in z_reps:
        varrived(z, 1)
        for r in y_reps:
            vsend(z, r, 1)
    for j in range(4, 7):
        keep(j)
    write(mixed, newmom_hbm, 4, 3)

    for r in y_reps + far_reps:
        varrived(r, 0)
    if EARLY:
        decode_chunks(0, EARLY, vals, iuv, (dth, dtl, dch, dcl), upd, (s_a, s_b), (v_a, v_b))
        write(upd, upd_hbm, 0, EARLY)
    for r in y_reps + far_reps:
        varrived(r, 1)
    for r in all_reps:
        varrived(r, 2)
    for cp in sends + vsends:
        cp.wait_send()
    for cp in outs:
        cp.wait()


def exchange(og, act, mom, idx):
    rows, cols = mom.shape[1:]
    tok = act.shape[1]
    table = dct_table()
    dt = np.kron(np.eye(4, dtype=np.float32), table.T)
    tables = split_table(dt) + split_table(dt.T.copy())
    ct2 = np.concatenate([table.T, table.T], axis=1)
    vmem = pl.BlockSpec(memory_space=pltpu.VMEM)
    anyw = pl.BlockSpec(memory_space=pl.ANY)
    S = jax.ShapeDtypeStruct
    return pl.pallas_call(
        exchange_kernel,
        out_shape=(
            S((rows, cols), f32),
            S((max(EARLY, 1) * 256, cols), bf16),
            S((16, 7, 8, 128), f32),
            S((28, 6, 8, 128), f32),
        ),
        in_specs=[anyw] * 9,
        out_specs=(anyw, anyw, vmem, vmem),
        scratch_shapes=[
            pltpu.VMEM((tok, rows), bf16),
            pltpu.VMEM((tok, cols), bf16),
            pltpu.VMEM((cols, rows), f32),
            pltpu.VMEM((rows, cols), f32),
            pltpu.VMEM(idx.shape, i32),
            pltpu.VMEM((42, 64, 128), f32),
            pltpu.VMEM((42, 128, 128), bf16),
            pltpu.VMEM((42, 128, 128), bf16),
            pltpu.VMEM((48, 128), f32),
        ]
        + [pltpu.VMEM((256, 256), bf16)] * 4
        + [
            pltpu.VMEM((64, 128), f32),
            pltpu.VMEM((max(EARLY, 1) * 256, cols), bf16),
            pltpu.VMEM((256, cols), f32),
            pltpu.VMEM((256, cols), f32),
            pltpu.VMEM((4, 4, 8, 128), f32),
            pltpu.VMEM((4, 4, 8, 128), f32),
            pltpu.SemaphoreType.DMA((10,)),
            pltpu.SemaphoreType.DMA((8 + 7 * PIECES,)),
            pltpu.SemaphoreType.DMA((16, PIECES)),
            pltpu.SemaphoreType.DMA((16,)),
            pltpu.SemaphoreType.DMA((45,)),
            pltpu.SemaphoreType.DMA((16, 3)),
            pltpu.SemaphoreType.DMA((3,)),
        ],
        compiler_params=pltpu.CompilerParams(collective_id=0, has_side_effects=True, vmem_limit_bytes=56 << 20),
        name="exchange",
    )(og, act, mom, idx, *tables, ct2)


def decode_chunks(first, last, vals, iuv, tables, update, s_bufs, v_bufs):
    dth, dtl, dch, dcl = tables
    io = lax.broadcasted_iota(i32, (64, 128), 0).astype(f32).astype(bf16)
    io2 = lax.broadcasted_iota(i32, (128, 128), 0).astype(f32).astype(bf16)
    zero, zero2 = jnp.zeros((64, 128), bf16), jnp.zeros((128, 128), bf16)
    one2 = jnp.ones((128, 128), bf16)
    lane = lax.broadcasted_iota(i32, (1, 128), 1)

    def spread(row, n):
        return jnp.broadcast_to(row, (n, 128)).astype(bf16)

    def scatter(j):
        s_buf, v_buf = s_bufs[j % 2], v_bufs[j % 2]
        for g in range(4):
            got = [vals[4 * i + g, j] for i in range(4)]
            for ai in range(4):
                v_buf[ai, g] = jnp.concatenate([v[:, 32 * ai : 32 * ai + 32] for v in got], axis=1)
        for ai in range(4):
            for bp in range(3):
                left, right = [], []
                for bo in range(2):
                    b = 2 * bp + bo
                    for g in range(4):
                        hit = spread(iuv[4 * j + ai, b, g : g + 1, :], 64) == io
                        v = v_buf[ai, g, b : b + 1, :]
                        vh = v.astype(bf16).astype(f32)
                        left.append(
                            jnp.concatenate(
                                [jnp.where(hit, spread(vh, 64), zero), jnp.where(hit, spread(v - vh, 64), zero)], axis=0
                            )
                        )
                        at = spread(iuv[4 * j + ai, b, 4 + g : 5 + g, :] + 64.0 * bo, 128)
                        right.append(jnp.where(at == io2, one2, zero2))
                o = dot_t(jnp.concatenate(left, axis=1), jnp.concatenate(right, axis=1))
                s_buf[64 * ai : 64 * ai + 64, 128 * bp : 128 * bp + 128] = o[:64] + o[64:]

    def inverse(j):
        sh, sl = split(s_bufs[j % 2][...])
        t = jnp.concatenate(
            [
                dot3(sh[:, :256], sl[:, :256], dch[...], dcl[...]),
                dot3(sh[:, 256:], sl[:, 256:], dch[:128, :128], dcl[:128, :128]),
            ],
            axis=1,
        )
        th, tl = split(t)
        d = dot3(dth[...], dtl[...], th, tl)
        for ai in range(4):
            for bp in range(3):
                blk = d[64 * ai : 64 * ai + 64, 128 * bp : 128 * bp + 128]
                col = jnp.sum(blk * blk, axis=0, keepdims=True)
                lo = jnp.sum(jnp.where(lane < 64, col, 0.0), axis=1, keepdims=True)
                hi = jnp.sum(jnp.where(lane < 64, 0.0, col), axis=1, keepdims=True)
                q = jnp.where(lane < 64, lo, hi) * (1.0 / (SPAN * SPAN))
                r0 = j * 256 + 64 * ai
                update[r0 : r0 + 64, 128 * bp : 128 * bp + 128] = jnp.tanh(blk * lax.rsqrt(q + 1e-06)).astype(bf16)

    scatter(first)
    for j in range(first, last):
        if j + 1 < last:
            scatter(j + 1)
        inverse(j)


def decode_kernel(
    newmom_in, upd_in, vals, iuv, dth, dtl, dch, dcl, newmom, update, m_buf, upd, s_a, s_b, v_a, v_b, sem
):
    rows = m_buf.shape[0]
    early = pl.ds(0, EARLY * 256)
    late = pl.ds(EARLY * 256, rows - EARLY * 256)
    m_in = pltpu.make_async_copy(newmom_in, m_buf, sem.at[0])
    m_out = pltpu.make_async_copy(m_buf, newmom.at[0], sem.at[1])
    m_in.start()
    if EARLY:
        u_in = pltpu.make_async_copy(upd_in, upd.at[early], sem.at[2])
        u_out = pltpu.make_async_copy(upd.at[early], update.at[early], sem.at[3])
        u_in.start()
    mid = EARLY + 1
    decode_chunks(EARLY, mid, vals, iuv, (dth, dtl, dch, dcl), upd, (s_a, s_b), (v_a, v_b))
    m_in.wait()
    m_out.start()
    if EARLY:
        u_in.wait()
        u_out.start()
    decode_chunks(mid, 7, vals, iuv, (dth, dtl, dch, dcl), upd, (s_a, s_b), (v_a, v_b))
    last = pltpu.make_async_copy(upd.at[late], update.at[late], sem.at[4])
    last.start()
    m_out.wait()
    if EARLY:
        u_out.wait()
    last.wait()


def decode(newmom, upd, vals, iuv):
    rows, cols = newmom.shape
    table = dct_table()
    dt = np.kron(np.eye(4, dtype=np.float32), table.T)
    tables = split_table(dt) + split_table(dt.T.copy())
    vmem = pl.BlockSpec(memory_space=pltpu.VMEM)
    anyw = pl.BlockSpec(memory_space=pl.ANY)
    S = jax.ShapeDtypeStruct
    return pl.pallas_call(
        decode_kernel,
        out_shape=(S((1, rows, cols), f32), S((rows, cols), bf16)),
        in_specs=[anyw] * 2 + [vmem] * 6,
        out_specs=(anyw, anyw),
        scratch_shapes=[
            pltpu.VMEM((rows, cols), f32),
            pltpu.VMEM((rows, cols), bf16),
            pltpu.VMEM((256, cols), f32),
            pltpu.VMEM((256, cols), f32),
            pltpu.VMEM((4, 4, 8, 128), f32),
            pltpu.VMEM((4, 4, 8, 128), f32),
            pltpu.SemaphoreType.DMA((5,)),
        ],
        compiler_params=pltpu.CompilerParams(vmem_limit_bytes=56 << 20),
        name="decode",
    )(newmom, upd, vals, iuv, *tables)


def per_device(hidden_act, out_grads, momentum, coeff_index):
    newmom, upd, vals, iuv = exchange(out_grads, hidden_act, momentum, coeff_index.transpose(1, 2, 0, 3))
    return decode(newmom, upd, vals, iuv)


def solution(mesh):
    placed = (
        P("rep", None, "tp"),
        P("rep", "tp", None),
        P("rep", "tp", None),
        P(None, "tp", None, None),
    )
    return jax.shard_map(
        per_device,
        mesh=mesh,
        in_specs=placed,
        out_specs=(P("rep", "tp", None), P("tp", None)),
        check_vma=False,
    )
```

time: 132 us -> 53.5 us (0.41)
  Pallas kernels: 128 us -> 52.6 us
  local copies, waits for them, and re-layouts: 3.02 us -> 0 us
    pallas_call x1, Pallas kernels: 87 us -> 10.1 us  [decode(): pl.pallas_call(decode_kernel, out_shape=(S((1, rows, cols), f32), S((rows...]
    unnamed x1 -> x0, local copies, waits for them, and re-layouts: 3.02 us -> none
where the time goes in v2:
time: 53.5 us; the launch traced here: 53.4 us
  Pallas kernels  52.6 us (98%)
  between operations  0.8 us (1%)
    pallas_call x1, Pallas kernels, exchange(): pl.pallas_call(exchange_kernel, out_shape=(S((rows, cols), f32), S((max(E...  42.5 us
    pallas_call x1, Pallas kernels, decode(): pl.pallas_call(decode_kernel, out_shape=(S((1, rows, cols), f32), S((rows...  10.1 us

profile of v2, /device:TPU:1, one launch (start us, length us, event | category | flops | bytes accessed | tf_op | source)
XLA Modules:
  0.0 53.4 jit_solution(10860940540471232062)
XLA Ops:
  0.6 42.5 %exchange.1 = (f32[1792,384]{1,0:T(8,128)}, bf16[512,384]{1,0:T(8,128)(2,1)}, f32[16,7,8,128]{3,2,1,0:T(8,128)}, f32[28,6,8,128]{3,2,1,0:T(8,128)}) custom-call(bf16[1,128,384]{2,1,0:T(8,128)(2,1)} %og_hbm.1, bf16[1,2048,1792]{2,1,0:T(8,128)(2,1)} %act_hbm.1, f32[1,1792,384]{2,1,0:T(8,128)} %mom_hbm.1, s32[28,6,16,32]{3,2,1,0:T(8,128)} %bitcast.1, ...), custom_call_target="tpu_custom_call" | custom-call | tf_op jit(solution)/shard_map/exchange/pallas_call | solution.py:358
  43.1 10.1 %decode.1 = (f32[1,1792,384]{2,1,0:T(8,128)}, bf16[1792,384]{1,0:T(8,128)(2,1)}) custom-call(f32[1792,384]{1,0:T(8,128)} %get-tuple-element.6.newmom_in, bf16[512,384]{1,0:T(8,128)(2,1)} %get-tuple-element.7.upd_in, f32[16,7,8,128]{3,2,1,0:T(8,128)} %get-tuple-element.8.vals, f32[28,6,8,128]{3,2,1,0:T(8,128)} %get-tuple-element.9.iuv, ...), custom_call_target="tpu_custom_call" | custom-call | tf_op jit(solution)/shard_map/decode/pallas_call | solution.py:501

commit v3 on v2

--- a/solution.py
+++ b/solution.py
@@ -53,9 +53,9 @@
 
 def exchange_kernel(
     og_hbm, act_hbm, mom_hbm, idx_hbm, dth_hbm, dtl_hbm, dch_hbm, dcl_hbm, ct2_hbm,
-    newmom_hbm, upd_hbm, vals, iuv,
-    act, og, gt, mixed, idx, cu, rh, rl, wrow, dth, dtl, dch, dcl, ct2, upd, s_a, s_b, v_a, v_b,
-    load_sem, og_send, og_recv, core_recv, v_send, v_recv, out_sem,
+    mixed, upd, vals, iuv,
+    act, og, gt, idx, cu, rh, rl, wrow, dth, dtl, dch, dcl, ct2, s_a, s_b, v_a, v_b,
+    load_sem, og_send, og_recv, core_recv, v_send, v_recv,
 ):
     rep, tp = lax.axis_index("rep"), lax.axis_index("tp")
     y, zl = rep // 4, rep % 4
@@ -217,6 +217,7 @@
             arrived(t, p)
         send_core(t)
     act_in[1].wait()
+
     mom_in.wait()
     for cp in table_in:
         cp.wait()
@@ -299,8 +300,6 @@
     for r in all_reps:
         vsend(rep, r, 2)
 
-    outs = []
-
     def keep(j):
         lane = lax.broadcasted_iota(i32, (64, 128), 1)
         for q in range(6):
@@ -313,36 +312,25 @@
             cols = slice(bp * 128, bp * 128 + 128)
             mixed[rows, cols] = mixed[rows, cols] - kept
 
-    def write(src, dst, lo, n):
-        rows = pl.ds(lo * 256, n * 256)
-        cp = pltpu.make_async_copy(src.at[rows], dst.at[rows], out_sem.at[len(outs)])
-        cp.start()
-        outs.append(cp)
-
     for j in range(4):
         keep(j)
-    write(mixed, newmom_hbm, 0, 4)
     for z in z_reps:
         varrived(z, 1)
         for r in y_reps:
             vsend(z, r, 1)
     for j in range(4, 7):
         keep(j)
-    write(mixed, newmom_hbm, 4, 3)
 
     for r in y_reps + far_reps:
         varrived(r, 0)
     if EARLY:
         decode_chunks(0, EARLY, vals, iuv, (dth, dtl, dch, dcl), upd, (s_a, s_b), (v_a, v_b))
-        write(upd, upd_hbm, 0, EARLY)
     for r in y_reps + far_reps:
         varrived(r, 1)
     for r in all_reps:
         varrived(r, 2)
     for cp in sends + vsends:
         cp.wait_send()
-    for cp in outs:
-        cp.wait()
 
 
 def exchange(og, act, mom, idx):
@@ -358,18 +346,17 @@
     return pl.pallas_call(
         exchange_kernel,
         out_shape=(
-            S((rows, cols), f32),
-            S((max(EARLY, 1) * 256, cols), bf16),
-            S((16, 7, 8, 128), f32),
-            S((28, 6, 8, 128), f32),
+            pltpu.VMEM((rows, cols), f32),
+            pltpu.VMEM((EARLY * 256, cols), bf16),
+            pltpu.VMEM((16, 7, 8, 128), f32),
+            pltpu.VMEM((28, 6, 8, 128), f32),
         ),
         in_specs=[anyw] * 9,
-        out_specs=(anyw, anyw, vmem, vmem),
+        out_specs=(vmem, vmem, vmem, vmem),
         scratch_shapes=[
             pltpu.VMEM((tok, rows), bf16),
             pltpu.VMEM((tok, cols), bf16),
             pltpu.VMEM((cols, rows), f32),
-            pltpu.VMEM((rows, cols), f32),
             pltpu.VMEM(idx.shape, i32),
             pltpu.VMEM((42, 64, 128), f32),
             pltpu.VMEM((42, 128, 128), bf16),
@@ -379,7 +366,6 @@
         + [pltpu.VMEM((256, 256), bf16)] * 4
         + [
             pltpu.VMEM((64, 128), f32),
-            pltpu.VMEM((max(EARLY, 1) * 256, cols), bf16),
             pltpu.VMEM((256, cols), f32),
             pltpu.VMEM((256, cols), f32),
             pltpu.VMEM((4, 4, 8, 128), f32),
@@ -390,14 +376,13 @@
             pltpu.SemaphoreType.DMA((16,)),
             pltpu.SemaphoreType.DMA((45,)),
             pltpu.SemaphoreType.DMA((16, 3)),
-            pltpu.SemaphoreType.DMA((3,)),
         ],
-        compiler_params=pltpu.CompilerParams(collective_id=0, has_side_effects=True, vmem_limit_bytes=56 << 20),
+        compiler_params=pltpu.CompilerParams(collective_id=0, has_side_effects=True, vmem_limit_bytes=57 << 20),
         name="exchange",
     )(og, act, mom, idx, *tables, ct2)
 
 
-def decode_chunks(first, last, vals, iuv, tables, update, s_bufs, v_bufs):
+def decode_chunks(first, last, vals, iuv, tables, update, s_bufs, v_bufs, ready=None, done=None):
     dth, dtl, dch, dcl = tables
     io = lax.broadcasted_iota(i32, (64, 128), 0).astype(f32).astype(bf16)
     io2 = lax.broadcasted_iota(i32, (128, 128), 0).astype(f32).astype(bf16)
@@ -455,39 +440,46 @@
                 update[r0 : r0 + 64, 128 * bp : 128 * bp + 128] = jnp.tanh(blk * lax.rsqrt(q + 1e-06)).astype(bf16)
 
     scatter(first)
+    if ready is not None:
+        ready()
     for j in range(first, last):
         if j + 1 < last:
             scatter(j + 1)
         inverse(j)
+        if done is not None:
+            done(j)
 
 
 def decode_kernel(
-    newmom_in, upd_in, vals, iuv, dth, dtl, dch, dcl, newmom, update, m_buf, upd, s_a, s_b, v_a, v_b, sem
+    newmom_in, upd_in, vals, iuv, dth_hbm, dtl_hbm, dch_hbm, dcl_hbm, newmom, update,
+    upd, dth, dtl, dch, dcl, s_a, s_b, v_a, v_b, sem,
 ):
-    rows = m_buf.shape[0]
+    tables = (dth, dtl, dch, dcl)
+    loads = [
+        pltpu.make_async_copy(src, dst, sem.at[9 + i])
+        for i, (src, dst) in enumerate(zip((dth_hbm, dtl_hbm, dch_hbm, dcl_hbm), tables))
+    ]
     early = pl.ds(0, EARLY * 256)
-    late = pl.ds(EARLY * 256, rows - EARLY * 256)
-    m_in = pltpu.make_async_copy(newmom_in, m_buf, sem.at[0])
-    m_out = pltpu.make_async_copy(m_buf, newmom.at[0], sem.at[1])
-    m_in.start()
-    if EARLY:
-        u_in = pltpu.make_async_copy(upd_in, upd.at[early], sem.at[2])
-        u_out = pltpu.make_async_copy(upd.at[early], update.at[early], sem.at[3])
-        u_in.start()
-    mid = EARLY + 1
-    decode_chunks(EARLY, mid, vals, iuv, (dth, dtl, dch, dcl), upd, (s_a, s_b), (v_a, v_b))
-    m_in.wait()
-    m_out.start()
-    if EARLY:
-        u_in.wait()
-        u_out.start()
-    decode_chunks(mid, 7, vals, iuv, (dth, dtl, dch, dcl), upd, (s_a, s_b), (v_a, v_b))
-    last = pltpu.make_async_copy(upd.at[late], update.at[late], sem.at[4])
-    last.start()
-    m_out.wait()
-    if EARLY:
-        u_out.wait()
-    last.wait()
+    outs = [
+        pltpu.make_async_copy(newmom_in, newmom.at[0], sem.at[7]),
+        pltpu.make_async_copy(upd_in, update.at[early], sem.at[8]),
+    ]
+    for cp in loads + outs:
+        cp.start()
+
+    def ready():
+        for cp in loads:
+            cp.wait()
+
+    def done(j):
+        rows = pl.ds(j * 256, 256)
+        cp = pltpu.make_async_copy(upd.at[rows], update.at[rows], sem.at[j])
+        cp.start()
+        outs.append(cp)
+
+    decode_chunks(EARLY, 7, vals, iuv, tables, upd, (s_a, s_b), (v_a, v_b), ready, done)
+    for cp in outs:
+        cp.wait()
 
 
 def decode(newmom, upd, vals, iuv):
@@ -501,25 +493,26 @@
     return pl.pallas_call(
         decode_kernel,
         out_shape=(S((1, rows, cols), f32), S((rows, cols), bf16)),
-        in_specs=[anyw] * 2 + [vmem] * 6,
+        in_specs=[vmem] * 4 + [anyw] * 4,
         out_specs=(anyw, anyw),
-        scratch_shapes=[
-            pltpu.VMEM((rows, cols), f32),
-            pltpu.VMEM((rows, cols), bf16),
+        scratch_shapes=[pltpu.VMEM((rows, cols), bf16)]
+        + [pltpu.VMEM((256, 256), bf16)] * 4
+        + [
             pltpu.VMEM((256, cols), f32),
             pltpu.VMEM((256, cols), f32),
             pltpu.VMEM((4, 4, 8, 128), f32),
             pltpu.VMEM((4, 4, 8, 128), f32),
-            pltpu.SemaphoreType.DMA((5,)),
+            pltpu.SemaphoreType.DMA((13,)),
         ],
-        compiler_params=pltpu.CompilerParams(vmem_limit_bytes=56 << 20),
+        compiler_params=pltpu.CompilerParams(vmem_limit_bytes=57 << 20),
         name="decode",
     )(newmom, upd, vals, iuv, *tables)
 
 
 def per_device(hidden_act, out_grads, momentum, coeff_index):
     newmom, upd, vals, iuv = exchange(out_grads, hidden_act, momentum, coeff_index.transpose(1, 2, 0, 3))
-    return decode(newmom, upd, vals, iuv)
+    held = [pltpu.with_memory_space_constraint(v, pltpu.VMEM) for v in (newmom, upd, vals, iuv)]
+    return decode(*held)
 
 
 def solution(mesh):

time: 53.5 us -> 50.6 us (0.946)
  Pallas kernels: 52.6 us -> 49.7 us
    pallas_call x1, Pallas kernels: 42.5 us -> 40.8 us  [exchange(): pl.pallas_call(exchange_kernel, out_shape=(pltpu.VMEM((rows, cols), f32),...]
    pallas_call x1, Pallas kernels: 10.1 us -> 8.87 us  [decode(): pl.pallas_call(decode_kernel, out_shape=(S((1, rows, cols), f32), S((rows...]
where the time goes in v3:
time: 50.6 us; the launch traced here: 50.5 us
  Pallas kernels  49.7 us (98%)
  between operations  0.8 us (2%)
    pallas_call x1, Pallas kernels, exchange(): pl.pallas_call(exchange_kernel, out_shape=(pltpu.VMEM((rows, cols), f32),...  40.8 us
    pallas_call x1, Pallas kernels, decode(): pl.pallas_call(decode_kernel, out_shape=(S((1, rows, cols), f32), S((rows...  8.87 us

profile of v3, /device:TPU:1, one launch (start us, length us, event | category | flops | bytes accessed | tf_op | source)
XLA Modules:
  0.0 50.5 jit_solution(4724534411430703566)
XLA Ops:
  0.6 40.8 %exchange.1 = (f32[1792,384]{1,0:T(8,128)S(1)}, bf16[512,384]{1,0:T(8,128)(2,1)S(1)}, f32[16,7,8,128]{3,2,1,0:T(8,128)S(1)}, f32[28,6,8,128]{3,2,1,0:T(8,128)S(1)}) custom-call(bf16[1,128,384]{2,1,0:T(8,128)(2,1)} %og_hbm.1, bf16[1,2048,1792]{2,1,0:T(8,128)(2,1)} %act_hbm.1, f32[1,1792,384]{2,1,0:T(8,128)} %mom_hbm.1, s32[28,6,16,32]{3,2,1,0:T(8,128)} %bitcast.1, ...), custom_call_target="tpu_custom_call" | custom-call | tf_op jit(solution)/shard_map/exchange/pallas_call | solution.py:346
  41.5 8.9 %decode.1 = (f32[1,1792,384]{2,1,0:T(8,128)}, bf16[1792,384]{1,0:T(8,128)(2,1)}) custom-call(f32[1792,384]{1,0:T(8,128)S(1)} %get-tuple-element.6.newmom_in, bf16[512,384]{1,0:T(8,128)(2,1)S(1)} %get-tuple-element.7.upd_in, f32[16,7,8,128]{3,2,1,0:T(8,128)S(1)} %get-tuple-element.8.vals, f32[28,6,8,128]{3,2,1,0:T(8,128)S(1)} %get-tuple-element.9.iuv, ...), custom_call_target="tpu_custom_call" | custom-call | tf_op jit(solution)/shard_map/decode/pallas_call | solution.py:493

commit v4 on v3

--- a/solution.py
+++ b/solution.py
@@ -108,12 +108,12 @@
     size = tok // PIECES
 
     def piece_copy(src_tp, dst_tp, p, k):
-        rows = pl.ds(pl.multiple_of(src_tp * tok + p * size, size), size)
+        rows = slot(src_tp) if p is None else pl.ds(pl.multiple_of(src_tp * tok + p * size, size), size)
         return pltpu.make_async_remote_copy(
             src_ref=og.at[rows],
             dst_ref=og.at[rows],
             send_sem=og_send.at[k],
-            recv_sem=og_recv.at[src_tp, p],
+            recv_sem=og_recv.at[src_tp, 0 if p is None else p],
             device_id=(rep, dst_tp),
             device_id_type=MESH,
         )
@@ -147,8 +147,8 @@
     og_in.wait()
     for p in range(PIECES):
         send(tp, z_peer, p)
-        for t in x_peers:
-            send(tp, t, p)
+    for t in x_peers:
+        send(tp, t, None)
     send_core(tp)
 
     idx_in.wait()
@@ -181,16 +181,15 @@
             rl[k] = cvl
         return 0
 
+    lax.fori_loop(0, 7, own_tables, 0)
+    for t in x_peers:
+        arrived(t, None)
+        send_core(t)
     for p in range(PIECES):
         arrived(z_peer, p)
         for t in x_peers:
             send(z_peer, t, p)
-        lax.fori_loop(7 * p // PIECES, 7 * (p + 1) // PIECES, own_tables, 0)
     send_core(z_peer)
-    for t in x_peers:
-        for p in range(PIECES):
-            arrived(t, p)
-        send_core(t)
 
     arrived_core(core_peer)
     for xx in xs:
@@ -218,6 +217,19 @@
         send_core(t)
     act_in[1].wait()
 
+    def late_slots(core):
+        return [slot(tpid(1 - zh, xx, core)) for xx in range(4)]
+
+    mine = late_slots(c)
+    bt1 = jnp.concatenate([og[r, :] for r in mine], axis=0).T
+
+    def late_grad(j, _):
+        cols = pl.ds(pl.multiple_of(j * 256, 256), 256)
+        gt[:, cols] = gt[:, cols] + dot(bt1, jnp.concatenate([act[r, cols] for r in mine], axis=0))
+        return 0
+
+    lax.fori_loop(0, 7, late_grad, 0)
+
     mom_in.wait()
     for cp in table_in:
         cp.wait()
@@ -225,33 +237,24 @@
     for xx in xs:
         arrived_core(tpid(1 - zh, xx, 1 - c))
 
-    off2 = pl.multiple_of((1 - zh) * half, half)
-    bt2 = og[pl.ds(off2, half), :].T
+    theirs = late_slots(1 - c)
+    bt2 = jnp.concatenate([og[r, :] for r in theirs], axis=0).T
 
     def forward(j):
         cols = slice(j * 256, j * 256 + 256)
-        g = gt[:, cols] + dot(bt2, act[pl.ds(off2, half), cols])
+        g = gt[:, cols] + dot(bt2, jnp.concatenate([act[r, cols] for r in theirs], axis=0))
         m = DECAY * mixed[cols, :] + g.T
         mixed[cols, :] = m
         mh, ml = split(m)
         lane = lax.broadcasted_iota(i32, (64, 128), 1)
         ws = []
-        hs = [dot3(mh[:, :256], ml[:, :256], dth[...], dtl[...])]
-        hs.append(dot3(mh[:, 256:], ml[:, 256:], dth[:128, :128], dtl[:128, :128]))
-        hs = [hs[0][:, :128], hs[0][:, 128:], hs[1]]
         for q in range(6):
             a2, bp = q // 3, q % 3
-            row = jnp.concatenate(
-                [
-                    (idx[4 * j + 2 * a2 + ap, 2 * bp + b, pl.ds(rep, 1), :] & 63) + 64 * b
-                    for ap in range(2)
-                    for b in range(2)
-                ],
-                axis=1,
-            )
-            ib = jnp.broadcast_to(row, (64, 128))
-            h = hs[bp][128 * a2 : 128 * a2 + 128]
-            got = jnp.where(lane < 64, lane_gather(h[:64], ib), lane_gather(h[64:], ib))
+            k = j * 6 + q
+            rows = slice(128 * a2, 128 * a2 + 128)
+            at = slice(128 * bp, 128 * bp + 128)
+            t = dot(mh[rows, at], rh[k]) + dot(ml[rows, at], rh[k]) + dot(mh[rows, at], rl[k])
+            got = jnp.where(lane < 64, t[:64], t[64:])
             w = jnp.sum(got * cu[j * 6 + q], axis=0, keepdims=True)
             wrow[j * 6 + q : j * 6 + q + 1, :] = w
             ws.append(w)
@@ -371,7 +374,7 @@
             pltpu.VMEM((4, 4, 8, 128), f32),
             pltpu.VMEM((4, 4, 8, 128), f32),
             pltpu.SemaphoreType.DMA((10,)),
-            pltpu.SemaphoreType.DMA((8 + 7 * PIECES,)),
+            pltpu.SemaphoreType.DMA((11 + 4 * PIECES,)),
             pltpu.SemaphoreType.DMA((16, PIECES)),
             pltpu.SemaphoreType.DMA((16,)),
             pltpu.SemaphoreType.DMA((45,)),

time: 50.6 us -> 48.5 us (0.958)
  Pallas kernels: 49.7 us -> 47.2 us
    pallas_call x1, Pallas kernels: 40.8 us -> 38.3 us  [exchange(): pl.pallas_call(exchange_kernel, out_shape=(pltpu.VMEM((rows, cols), f32),...]
where the time goes in v4:
time: 48.5 us; the launch traced here: 48 us
  Pallas kernels  47.2 us (97%)
  between operations  0.8 us (2%)
    pallas_call x1, Pallas kernels, exchange(): pl.pallas_call(exchange_kernel, out_shape=(pltpu.VMEM((rows, cols), f32),...  38.3 us
    pallas_call x1, Pallas kernels, decode(): pl.pallas_call(decode_kernel, out_shape=(S((1, rows, cols), f32), S((rows...  8.87 us

profile of v4, /device:TPU:1, one launch (start us, length us, event | category | flops | bytes accessed | tf_op | source)
XLA Modules:
  0.0 48.0 jit_solution(5026630169286245554)
XLA Ops:
  0.6 38.3 %exchange.1 = (f32[1792,384]{1,0:T(8,128)S(1)}, bf16[512,384]{1,0:T(8,128)(2,1)S(1)}, f32[16,7,8,128]{3,2,1,0:T(8,128)S(1)}, f32[28,6,8,128]{3,2,1,0:T(8,128)S(1)}) custom-call(bf16[1,128,384]{2,1,0:T(8,128)(2,1)} %og_hbm.1, bf16[1,2048,1792]{2,1,0:T(8,128)(2,1)} %act_hbm.1, f32[1,1792,384]{2,1,0:T(8,128)} %mom_hbm.1, s32[28,6,16,32]{3,2,1,0:T(8,128)} %bitcast.1, ...), custom_call_target="tpu_custom_call" | custom-call | tf_op jit(solution)/shard_map/exchange/pallas_call | solution.py:349
  39.0 8.9 %decode.1 = (f32[1,1792,384]{2,1,0:T(8,128)}, bf16[1792,384]{1,0:T(8,128)(2,1)}) custom-call(f32[1792,384]{1,0:T(8,128)S(1)} %get-tuple-element.6.newmom_in, bf16[512,384]{1,0:T(8,128)(2,1)S(1)} %get-tuple-element.7.upd_in, f32[16,7,8,128]{3,2,1,0:T(8,128)S(1)} %get-tuple-element.8.vals, f32[28,6,8,128]{3,2,1,0:T(8,128)S(1)} %get-tuple-element.9.iuv, ...), custom_call_target="tpu_custom_call" | custom-call | tf_op jit(solution)/shard_map/decode/pallas_call | solution.py:496

commit v5 on v4

--- a/solution.py
+++ b/solution.py
@@ -12,7 +12,7 @@
 SPAN = 64
 DECAY = 0.9
 PIECES = 4
-EARLY = 2
+EARLY = 3
 MESH = pl.DeviceIdType.MESH
 f32, bf16, i32 = jnp.float32, jnp.bfloat16, jnp.int32
 
@@ -72,7 +72,7 @@
     z_reps = [y * 4 + lax.rem(zl + d, 4) for d in (1, 2, 3)]
     y_reps = [lax.rem(y + d, 4) * 4 + zl for d in (1, 3, 2)]
     far_reps = [lax.rem(y + d, 4) * 4 + lax.rem(zl + e, 4) for d in (1, 3, 2) for e in (1, 2, 3)]
-    all_reps = z_reps + y_reps + far_reps
+    all_reps = z_reps + y_reps
 
     barrier = pltpu.get_barrier_semaphore()
     for t in x_peers + [core_peer, z_peer]:
@@ -323,6 +323,10 @@
             vsend(z, r, 1)
     for j in range(4, 7):
         keep(j)
+    for z in z_reps:
+        varrived(z, 2)
+        for r in y_reps:
+            vsend(z, r, 2)
 
     for r in y_reps + far_reps:
         varrived(r, 0)
@@ -330,7 +334,7 @@
         decode_chunks(0, EARLY, vals, iuv, (dth, dtl, dch, dcl), upd, (s_a, s_b), (v_a, v_b))
     for r in y_reps + far_reps:
         varrived(r, 1)
-    for r in all_reps:
+    for r in y_reps + far_reps:
         varrived(r, 2)
     for cp in sends + vsends:
         cp.wait_send()

time: 48.5 us -> 48.8 us (level)
  the two profiles are of different devices: /device:TPU:1 before, /device:TPU:32 now
where the time goes in v5:
time: 48.8 us; the launch traced here: 48.7 us
  Pallas kernels  47.9 us (98%)
  between operations  0.8 us (2%)
    pallas_call x1, Pallas kernels, exchange(): pl.pallas_call(exchange_kernel, out_shape=(pltpu.VMEM((rows, cols), f32),...  40.4 us
    pallas_call x1, Pallas kernels, decode(): pl.pallas_call(decode_kernel, out_shape=(S((1, rows, cols), f32), S((rows...  7.43 us

profile of v5, /device:TPU:32, one launch (start us, length us, event | category | flops | bytes accessed | tf_op | source)
XLA Modules:
  0.0 48.7 jit_solution(175185089454842326)
XLA Ops:
  0.6 40.4 %exchange.1 = (f32[1792,384]{1,0:T(8,128)S(1)}, bf16[768,384]{1,0:T(8,128)(2,1)S(1)}, f32[16,7,8,128]{3,2,1,0:T(8,128)S(1)}, f32[28,6,8,128]{3,2,1,0:T(8,128)S(1)}) custom-call(bf16[1,128,384]{2,1,0:T(8,128)(2,1)} %og_hbm.1, bf16[1,2048,1792]{2,1,0:T(8,128)(2,1)} %act_hbm.1, f32[1,1792,384]{2,1,0:T(8,128)} %mom_hbm.1, s32[28,6,16,32]{3,2,1,0:T(8,128)} %bitcast.1, ...), custom_call_target="tpu_custom_call" | custom-call | tf_op jit(solution)/shard_map/exchange/pallas_call | solution.py:353
  41.1 7.4 %decode.1 = (f32[1,1792,384]{2,1,0:T(8,128)}, bf16[1792,384]{1,0:T(8,128)(2,1)}) custom-call(f32[1792,384]{1,0:T(8,128)S(1)} %get-tuple-element.6.newmom_in, bf16[768,384]{1,0:T(8,128)(2,1)S(1)} %get-tuple-element.7.upd_in, f32[16,7,8,128]{3,2,1,0:T(8,128)S(1)} %get-tuple-element.8.vals, f32[28,6,8,128]{3,2,1,0:T(8,128)S(1)} %get-tuple-element.9.iuv, ...), custom_call_target="tpu_custom_call" | custom-call | tf_op jit(solution)/shard_map/decode/pallas_call | solution.py:500
